TPU v7x, 32 devices: a whole 2x2x4 slice. The times are simulated.
32 devices in a mesh: net: 8 (over z, y), scen: 4 (over x, core).
Axes of the slice: x: 2, y: 2, z: 4, core: 2. Of those that a mesh axis runs over, the one named last changes fastest.
Arguments:
- volt_mag: float32 [1920, 8], P('net', 'scen'), parts along dimension 1, may hold values from 0.94 to 1.06
- volt_ang: float32 [1920, 8], P('net', 'scen'), parts along dimension 1, may hold values from -0.5 to 0.5
- gradient: float32 [1920, 2, 8], P('net', None, 'scen'), parts along dimension 2, may hold values from -40 to 40
- branch_from: int32 [2560], P('net'), may hold values from 0 to 239, as said below
- branch_to: int32 [2560], P('net'), may hold values from 0 to 479, as said below
- branch_count: int32 [8], P('net'), may hold values from 160 to 320, as said below
- boundary: int32 [1920], P('net'), may hold values from 0 to 239, as said below
- conductance: float32 [2560], P('net'), may hold values from 0.2 to 2
- susceptance: float32 [2560], P('net'), may hold values from 1 to 10
- duals: float32 [2, 2560, 8], P(None, 'net', 'scen'), parts along dimension 2, may hold values from 0.02 to 0.2
- slacks: float32 [2, 2560, 8], P(None, 'net', 'scen'), parts along dimension 2, may hold values from 0.2 to 2
- gen_bus: int32 [320], P('net'), may hold values from 0 to 239
- gen_curvature: float32 [320], P('net'), may hold values from 1 to 10
Outputs:
- search_step: float32 [1920, 2, 8], P('net', None, 'scen'), parts along dimension 2
- residual: float32 [1920, 2, 8], P('net', None, 'scen'), parts along dimension 2
There are 4 independent parts, one for each index of `scen`. A program takes and returns all parts, laid end to end along the dimension named above; an argument that names none is the same for every part. Nothing has to cross between parts.
Inputs may be any that keep to these rules, and one draw needn't show every extreme that they name: `branch_from`: A bus index within the branch's own device. A branch whose branch_to is 240 + e with e >= 0 starts at boundary entry e of its own device. `branch_to`: below 240: a bus of the same device other than the from-bus. 240 + e for e < 120: entry e of the previous device's list toward this device; 360 + e: entry e of the next device's list toward this device. Only the first 240 slots of a device end at a neighbour, each such value at most once a device; the first device has no ends of the first kind, the last none of the second. `branch_count`: slots at or past a device's count contribute nothing. Some device is full in every draw. `boundary`: per device 2 * 120 distinct local buses: the first 120 face the previous device, the rest the next device.
All inputs are finite; a program needn't handle non-finite values.
Results may differ from a plain program's by a relative error of at most 0.0003.
Values sent between devices are 32-bit elements; how exact they have to be, the bound alone decides.
No kernel may reach another device: no remote copies, remote signals or barrier semaphores. Data moves between devices by JAX's collectives and lax.ppermute only.
A program may use at most 64 MiB of HBM per device.

v0:
```python
import functools

import jax
import jax.numpy as jnp
from jax import lax
from jax.experimental import pallas as pl
from jax.experimental.pallas import tpu as pltpu
from jax.sharding import PartitionSpec as P

ITERS = 4


barrier_weight = 0.01
volt_low = 0.9
volt_high = 1.1
angle_reg = 0.5


def shifted(array, axis, by):
    peers = lax.axis_size(axis)
    pairs = [(i, i + by) for i in range(peers) if 0 <= i + by < peers]
    return lax.ppermute(array, axis, pairs)


def branch_blocks(
    magnitude_from,
    angle_from,
    magnitude_to,
    angle_to,
    conduct,
    suscept,
    weight_active,
    weight_reactive,
):
    angle_diff = angle_from - angle_to
    cosine_diff = jnp.cos(angle_diff)
    sine_diff = jnp.sin(angle_diff)
    flow_along = conduct * cosine_diff + suscept * sine_diff
    flow_across = conduct * sine_diff - suscept * cosine_diff
    cross_term = magnitude_from * magnitude_to
    active_rows = (
        2.0 * conduct * magnitude_from - magnitude_to * flow_along,
        cross_term * flow_across,
        -magnitude_from * flow_along,
        -cross_term * flow_across,
    )
    reactive_rows = (
        -2.0 * suscept * magnitude_from - magnitude_to * flow_across,
        -cross_term * flow_along,
        -magnitude_from * flow_across,
        cross_term * flow_along,
    )

    def block_entry(left_index, right_index):
        return (
            weight_active * active_rows[left_index] * active_rows[right_index]
            + weight_reactive * reactive_rows[left_index] * reactive_rows[right_index]
        )

    from_block = jnp.stack([block_entry(0, 0), block_entry(0, 1), block_entry(1, 1)], axis=1)
    to_block = jnp.stack([block_entry(2, 2), block_entry(2, 3), block_entry(3, 3)], axis=1)
    cross_block = jnp.stack(
        [block_entry(0, 2), block_entry(0, 3), block_entry(1, 2), block_entry(1, 3)], axis=1
    )
    return (from_block, to_block, cross_block)


def apply_cross(matrix_block, vector):
    return jnp.stack(
        [
            matrix_block[:, 0] * vector[:, 0] + matrix_block[:, 1] * vector[:, 1],
            matrix_block[:, 2] * vector[:, 0] + matrix_block[:, 3] * vector[:, 1],
        ],
        axis=1,
    )


def apply_cross_transposed(matrix_block, vector):
    return jnp.stack(
        [
            matrix_block[:, 0] * vector[:, 0] + matrix_block[:, 2] * vector[:, 1],
            matrix_block[:, 1] * vector[:, 0] + matrix_block[:, 3] * vector[:, 1],
        ],
        axis=1,
    )


def scenario_sum(left_vec, right_vec):
    return jnp.sum(left_vec * right_vec, axis=(0, 1))


def widen(values):
    return values[None, None, :]


def body(
    volt_mag,
    volt_ang,
    gradient,
    branch_from,
    branch_to,
    branch_count,
    boundary,
    conductance,
    susceptance,
    duals,
    slacks,
    gen_bus,
    gen_curvature,
):
    bus_count = volt_mag.shape[0]
    ghost_count = boundary.shape[0] // 2
    extended_size = bus_count + 2 * ghost_count
    slot_count = branch_from.shape[0]
    left_list = boundary[:ghost_count]
    right_list = boundary[ghost_count:]
    left_ghost = slice(bus_count, bus_count + ghost_count)
    right_ghost = slice(bus_count + ghost_count, extended_size)
    return_plan = (
        (-1, left_ghost, right_list, right_ghost),
        (1, right_ghost, left_list, left_ghost),
    )

    def share_vector(values):
        pieces = [values]
        for direction in (1, -1):
            outgoing = jnp.take(values, right_list if direction == 1 else left_list, axis=0)
            pieces.append(shifted(outgoing, "net", direction))
        return jnp.concatenate(pieces, axis=0)

    bus_state = jnp.stack([volt_mag, volt_ang], axis=1)
    pieces = [bus_state]
    for share_direction in (1, -1):
        outgoing = jnp.take(bus_state, right_list if share_direction == 1 else left_list, axis=0)
        pieces.append(shifted(outgoing, "net", share_direction))
    extended_state = jnp.concatenate(pieces, axis=0)
    from_state = jnp.take(extended_state, branch_from, axis=0)
    to_state = jnp.take(extended_state, branch_to, axis=0)
    live_mask = (jnp.arange(slot_count) < branch_count[0]).astype(jnp.float32)[:, None]
    weight_active = live_mask * duals[0] / slacks[0]
    weight_reactive = live_mask * duals[1] / slacks[1]
    from_block, to_block, cross_block = branch_blocks(
        from_state[:, 0],
        from_state[:, 1],
        to_state[:, 0],
        to_state[:, 1],
        conductance[:, None],
        susceptance[:, None],
        weight_active,
        weight_reactive,
    )
    diag_extended = jax.ops.segment_sum(
        from_block, branch_from, num_segments=extended_size
    ) + jax.ops.segment_sum(to_block, branch_to, num_segments=extended_size)
    diag_local = diag_extended[:bus_count]
    for direction, ghost_rows, target_rows, source_rows in return_plan:
        arrived_diag = shifted(diag_extended[ghost_rows], "net", direction)
        diag_local = diag_local.at[target_rows].add(arrived_diag)
    gen_table = (gen_bus[None, :] == jnp.arange(bus_count)[:, None]).astype(jnp.float32)
    gen_sum = jnp.dot(gen_table, gen_curvature, precision=lax.Precision.HIGHEST)[:, None]
    barrier = barrier_weight / jnp.square(volt_mag - volt_low) + barrier_weight / jnp.square(
        volt_high - volt_mag
    )
    diag_vv = diag_local[:, 0] + barrier + gen_sum
    diag_va = diag_local[:, 1]
    diag_aa = diag_local[:, 2] + angle_reg + gen_sum
    determinant = diag_vv * diag_aa - diag_va * diag_va
    inverse_vv = diag_aa / determinant
    inverse_va = -diag_va / determinant
    inverse_aa = diag_vv / determinant

    def precondition(vector):
        return jnp.stack(
            [
                inverse_vv * vector[:, 0] + inverse_va * vector[:, 1],
                inverse_va * vector[:, 0] + inverse_aa * vector[:, 1],
            ],
            axis=1,
        )

    update_field = jnp.zeros_like(gradient)
    residual = gradient

    def energy_of(residual_now, scaled_now):
        return lax.psum(scenario_sum(residual_now, scaled_now), "net")

    scaled = precondition(residual)
    search = scaled
    energy = energy_of(residual, scaled)
    for iteration in range(ITERS):
        extended = share_vector(search)
        from_values = jnp.take(extended, branch_from, axis=0)
        to_values = jnp.take(extended, branch_to, axis=0)
        from_terms = apply_cross(cross_block, to_values)
        to_terms = apply_cross_transposed(cross_block, from_values)
        result = jnp.stack(
            [
                diag_vv * search[:, 0] + diag_va * search[:, 1],
                diag_va * search[:, 0] + diag_aa * search[:, 1],
            ],
            axis=1,
        )
        summed = jax.ops.segment_sum(
            from_terms, branch_from, num_segments=extended_size
        ) + jax.ops.segment_sum(to_terms, branch_to, num_segments=extended_size)
        local_sum = result + summed[:bus_count]
        for apply_direction, apply_ghost_rows, apply_target_rows, apply_source_rows in return_plan:
            arrived = shifted(summed[apply_ghost_rows], "net", apply_direction)
            local_sum = local_sum.at[apply_target_rows].add(arrived)
        step_size = energy / lax.psum(scenario_sum(search, local_sum), "net")
        update_field = update_field + widen(step_size) * search
        residual = residual - widen(step_size) * local_sum
        if iteration + 1 < ITERS:
            scaled = precondition(residual)
            energy_next = energy_of(residual, scaled)
            search = scaled + widen(energy_next / energy) * search
            energy = energy_next
    return (update_field, residual)


LANES = 128
ROWS = 8
TILE_A, TILE_B, TILE_C = 0, 2, 4
TILE_LOCAL = 6
TILE_INDEX = 9
PAYLOAD_ROWS = 11 * ROWS
CHUNK_FIELDS = ["gradient", "diag", "diag_off", "vm", "cosv", "sinv"]
CHUNK_FIELDS += ["wp", "wq", "g", "b", "extent"]
SLOT_FIELDS = ["local_main", "local_off", "at_from", "at_to"]
SET_RANKS = 4
SET_RANKS_OUTER = 6


def fits_fast_path(blocks, bus_count, ghost_count, slot_count, gen_count, scen_count):
    return (
        blocks == 8
        and scen_count == 2
        and bus_count == 2 * ghost_count
        and ghost_count <= LANES
        and 2 * LANES < slot_count < 3 * LANES
        and gen_count <= LANES
    )


def iota(shape, dim):
    return lax.broadcasted_iota(jnp.int32, shape, dim)


def lane_take(table, index):
    return jnp.take_along_axis(table, index, axis=1, mode="promise_in_bounds")


def take_chunks(tables, index):
    lane = index & (LANES - 1)
    chunk = index >> 7
    out = lane_take(tables[0], lane)
    for number in range(1, len(tables)):
        out = jnp.where(chunk == number, lane_take(tables[number], lane), out)
    return out


def take_listed(tables, index, default=0):
    lane = index & (LANES - 1)
    chunk = index >> 7
    out = jnp.full(index.shape, default, tables[0].dtype)
    for number, table in enumerate(tables):
        out = jnp.where(chunk == number, lane_take(table, lane), out)
    return out


def tall(row):
    return jnp.broadcast_to(row, (ROWS, LANES))


def column(row):
    return jnp.transpose(jnp.broadcast_to(row, (LANES, LANES)))


def block_entries(vi, ci, si, vj, cj, sj, g, b, wp, wq):
    cosine = ci * cj + si * sj
    sine = si * cj - ci * sj
    along = g * cosine + b * sine
    across = g * sine - b * cosine
    cross = vi * vj
    p0 = 2.0 * g * vi - vj * along
    p1 = cross * across
    p2 = -vi * along
    q0 = -2.0 * b * vi - vj * across
    q1 = -cross * along
    q2 = -vi * across

    def entry(pa, pb, qa, qb):
        return wp * pa * pb + wq * qa * qb

    return (
        entry(p0, p0, q0, q0),
        entry(p0, p1, q0, q1),
        entry(p1, p1, q1, q1),
        entry(p2, p2, q2, q2),
        entry(p1, p2, q1, q2),
        entry(p0, p2, q0, q2),
    )


def prepare_kernel(
    vm_ref,
    va_ref,
    grad_ref,
    from_ref,
    to_ref,
    count_ref,
    bound_ref,
    g_ref,
    b_ref,
    duals_ref,
    slacks_ref,
    gen_bus_ref,
    gen_curv_ref,
    out_ref,
    pos_ref,
    bus_scr,
    branch_scr,
    index_scr,
):
    bus_count = vm_ref.shape[1]
    ghost_count = bus_count // 2
    slot_count = from_ref.shape[0]
    gen_count = gen_bus_ref.shape[0]
    none = 3 * LANES - 1
    live_count = count_ref[...][None]

    bus_scr[...] = jnp.zeros_like(bus_scr)
    branch_scr[...] = jnp.zeros_like(branch_scr)
    index_scr[...] = jnp.full_like(index_scr, -9)
    for copy in range(4):
        bus_scr[2 * copy : 2 * copy + 2, :bus_count] = vm_ref[...]
        bus_scr[8 + 2 * copy : 10 + 2 * copy, :bus_count] = va_ref[...]
    for comp in range(2):
        bus_scr[16 + 2 * comp : 18 + 2 * comp, :bus_count] = grad_ref[comp]
    live = iota((2, slot_count), 1) < live_count
    for kind in range(2):
        weight = jnp.where(live, duals_ref[kind] / slacks_ref[kind], 0.0)
        branch_scr[2 * kind : 2 * kind + 2, :slot_count] = weight
    branch_scr[4:5, :slot_count] = g_ref[...][None]
    branch_scr[5:6, :slot_count] = b_ref[...][None]
    branch_scr[6:7, :slot_count] = from_ref[...][None].astype(jnp.float32)
    branch_scr[7:8, :slot_count] = to_ref[...][None].astype(jnp.float32)
    bus_scr[20:21, :gen_count] = gen_curv_ref[...][None]
    index_scr[0:1, :slot_count] = from_ref[...][None]
    index_scr[1:2, :slot_count] = to_ref[...][None]
    index_scr[2:3, :bus_count] = bound_ref[...][None]
    index_scr[3:4, :gen_count] = gen_bus_ref[...][None]

    def tiles(ref, first, chunks):
        return [ref[first : first + ROWS, LANES * c : LANES * (c + 1)] for c in range(chunks)]

    def row(ref, number, chunk):
        return ref[number : number + 1, LANES * chunk : LANES * (chunk + 1)]

    lane = iota((ROWS, LANES), 1)
    sub = iota((ROWS, LANES), 0)
    lane_row = iota((1, LANES), 1)
    sub_col = iota((LANES, LANES), 0).astype(jnp.float32)
    inside = lane < ghost_count

    raw_bound = [tall(row(index_scr, 2, c)) for c in range(2)]
    bound = [jnp.where(inside, take_chunks(raw_bound, lane + h * ghost_count), -1) for h in range(2)]
    fetch = [jnp.maximum(b, 0) for b in bound]
    bound_row = [b[0:1].astype(jnp.float32) for b in bound]
    vm_raw, va_raw, grad_raw = (tiles(bus_scr, 8 * f, 2) for f in range(3))
    vm = [jnp.where(inside, take_chunks(vm_raw, f), 1.0) for f in fetch]
    va = [jnp.where(inside, take_chunks(va_raw, f), 0.0) for f in fetch]
    grad = [jnp.where(inside, take_chunks(grad_raw, f), 0.0) for f in fetch]
    cosv = [jnp.cos(a) for a in va]
    sinv = [jnp.sin(a) for a in va]

    earlier = (iota((LANES, LANES), 0) < iota((LANES, LANES), 1)).astype(jnp.bfloat16)
    local, cross_key, place = [], [], []
    local_count = jnp.zeros((1, 1), jnp.float32)
    for c in range(3):
        slot = lane_row + LANES * c
        alive = (slot < live_count) & (slot < slot_count)
        to_raw = row(index_scr, 1, c)
        cross_key.append(jnp.where(alive, to_raw, 9999).astype(jnp.float32))
        keep = jnp.where(alive & (to_raw < bus_count), 1.0, 0.0)
        before = jnp.dot(
            tall(keep).astype(jnp.bfloat16), earlier, preferred_element_type=jnp.float32
        )
        place.append(jnp.where(keep > 0.0, before[0:1] + local_count, -1.0))
        local_count = local_count + jnp.sum(keep, axis=1, keepdims=True)
    place_col = [column(p) for p in place]
    lane_f = lane_row.astype(jnp.float32)
    branch_tiles = tiles(branch_scr, 0, 3)

    def lowest(masks):
        found = functools.reduce(
            jnp.minimum,
            [jnp.where(m, sub_col + float(LANES * c), float(none)) for c, m in masks],
        )
        return jnp.min(found, axis=0, keepdims=True)

    packed, from_key, to_key = [], [], []
    for c in range(3):
        source = lowest([(d, place_col[d] == lane_f + float(LANES * c)) for d in range(c, 3)])
        tile = take_chunks(branch_tiles, tall(source).astype(jnp.int32))
        packed.append(tile)
        empty = source == float(none)
        from_key.append(jnp.where(empty, 9998.0, tile[6:7]))
        to_key.append(jnp.where(empty, 9999.0, tile[7:8]))
    from_col = [column(k) for k in from_key]
    to_col = [column(k) for k in to_key]
    cross_col = [column(k) for k in cross_key[:2]]
    bound_col = [column(b) for b in bound_row]
    gen_col = column(row(index_scr, 3, 0).astype(jnp.float32))
    curv_col = column(row(bus_scr, 20, 0))

    def links(keys, cols):
        heads, counts, matches = [], [], []
        for h in range(2):
            equal = [cols[c] == bound_row[h] for c in range(3)]
            matches.append([jnp.where(e, 1.0, 0.0).astype(jnp.bfloat16) for e in equal])
            heads.append(lowest(list(enumerate(equal))))
            counts.append(
                jnp.sum(
                    functools.reduce(jnp.add, [jnp.where(e, 1.0, 0.0) for e in equal]),
                    axis=0,
                    keepdims=True,
                )
            )
        nexts = []
        for c in range(3):
            later = [(c, (cols[c] == keys[c]) & (sub_col > lane_f))]
            later += [(d, cols[d] == keys[c]) for d in range(c + 1, 3)]
            nexts.append(lowest(later))
        return heads, nexts, jnp.maximum(counts[0], counts[1]), matches

    head_f, next_f, count_f, match_f = links(from_key, from_col)
    head_t, next_t, count_t, match_t = links(to_key, to_col)
    degree = jnp.max(jnp.maximum(count_f, count_t))

    def position(keys):
        found = [
            jnp.where(bound_col[h] == keys, sub_col + float(LANES * h), 0.0) for h in range(2)
        ]
        return jnp.max(jnp.maximum(found[0], found[1]), axis=0, keepdims=True)

    pos_f = [position(k) for k in from_key]
    pos_t = [position(k) for k in to_key]
    for m in range(2):
        pos_ref[m : m + 1, :] = position((lane_row + LANES * m).astype(jnp.float32)).astype(jnp.int32)

    cross = []
    for h in range(2):
        target = jnp.where(lane_row < ghost_count, bus_count + h * ghost_count + lane_row, -5)
        slot = lowest([(c, cross_col[c] == target.astype(jnp.float32)) for c in range(2)])
        cross.append(take_chunks(branch_tiles, tall(slot).astype(jnp.int32)))

    gens = [
        jnp.sum(jnp.where(gen_col == bound_row[h], curv_col, 0.0), axis=0, keepdims=True)
        for h in range(2)
    ]

    pair = sub & 3

    def every_pair(x):
        x = jnp.where(sub < 2, x, pltpu.roll(x, 2, 0))
        return jnp.where(sub < 4, x, pltpu.roll(x, 4, 0))

    from_table, to_table = [], []
    for c in range(3):
        at_f = tall(pos_f[c]).astype(jnp.int32)
        at_t = tall(pos_t[c]).astype(jnp.int32)
        h00, h01, h11, h22, h12, h02 = block_entries(
            *(take_chunks(t, at_f) for t in (vm, cosv, sinv)),
            *(take_chunks(t, at_t) for t in (vm, cosv, sinv)),
            tall(packed[c][4:5]),
            tall(packed[c][5:6]),
            every_pair(packed[c]),
            every_pair(pltpu.roll(packed[c], 6, 0)),
        )
        main = jnp.where(pair < 2, h02, -h11)
        off = jnp.where(pair < 2, -h01, h12)
        first = ROWS * (TILE_LOCAL + c)
        out_ref[first : first + ROWS, :] = jnp.where(sub < 4, main, off)
        from_table.append(jnp.where(sub < 2, h00, jnp.where(sub < 4, h01, h11)))
        to_table.append(jnp.where(sub < 2, h22, jnp.where(sub < 4, -h12, h11)))

    def parts(x):
        high = x.astype(jnp.bfloat16).astype(jnp.float32)
        middle = (x - high).astype(jnp.bfloat16).astype(jnp.float32)
        rest = x - high - middle
        return jnp.concatenate([high, middle, rest, jnp.zeros_like(x)], axis=0).astype(jnp.bfloat16)

    terms = [parts(t) for t in from_table + to_table]
    acc = []
    for h in range(2):
        total = functools.reduce(
            jnp.add,
            [
                jnp.dot(term, match, preferred_element_type=jnp.float32)
                for term, match in zip(terms, match_f[h] + match_t[h])
            ],
        )
        acc.append(total[0:8] + total[8:16] + total[16:24])

    total_local = jnp.max(local_count)

    for h in range(2):
        below = vm[h] - volt_low
        above = volt_high - vm[h]
        barrier = barrier_weight / (below * below) + barrier_weight / (above * above)
        diag_vv = pltpu.roll(acc[h], 4, 0) + barrier + gens[h]
        diag_aa = pltpu.roll(acc[h], 2, 0) + angle_reg + gens[h]
        diag_va = pltpu.roll(acc[h], 6, 0)
        first = ROWS * (TILE_A + h)
        out_ref[first : first + ROWS, :] = jnp.where(
            sub < 4, grad[h], jnp.where(sub < 6, diag_vv, diag_aa)
        )
        first = ROWS * (TILE_B + h)
        out_ref[first : first + ROWS, :] = jnp.where(
            sub < 2, diag_va, jnp.where(sub < 4, vm[h], jnp.where(sub < 6, cosv[h], sinv[h]))
        )
        first = ROWS * (TILE_C + h)
        out_ref[first : first + ROWS, :] = jnp.where(
            sub < 6, cross[h], jnp.where(sub == 6, degree, total_local)
        )
    first = ROWS * TILE_INDEX
    for offset, value in enumerate(pos_f + pos_t + head_f + head_t + next_f + next_t):
        out_ref[first + offset : first + offset + 1, :] = value


def solve_kernel(me_ref, pos_ref, *refs):
    *all_refs, step_ref, residual_ref, chain_scr, row_scr, field_scr, step_scr, residual_scr = refs
    blocks = len(all_refs)
    me = me_ref[0]
    half = blocks // 2
    bus_count = step_ref.shape[2]
    lane_pairs = [(j, h) for j in range(half) for h in range(2)]
    sub = iota((ROWS, LANES), 0)
    low = sub < 4
    even = (sub & 3) < 2

    def swap_component(x):
        return jnp.where(even, pltpu.roll(x, 6, 0), pltpu.roll(x, 2, 0))

    def swap_block(x):
        return pltpu.roll(x, 4, 0)

    upper = me >= half
    mine = jnp.where(upper, blocks - 1 - me, me)
    near = low != upper

    def halves(tile, j):
        here = all_refs[j][ROWS * tile : ROWS * (tile + 1), :]
        there = all_refs[blocks - 1 - j][ROWS * tile : ROWS * (tile + 1), :]
        first = jnp.where(upper, there, here)
        second = jnp.where(upper, here, there)
        return (
            jnp.where(low, first, swap_block(second)),
            jnp.where(low, swap_block(first), second),
        )

    def quarters(x):
        return (
            jnp.where(even, x, pltpu.roll(x, 2, 0)),
            jnp.where(even, pltpu.roll(x, 6, 0), x),
        )

    def single(number, j):
        return jnp.where(
            near,
            tall(all_refs[j][number : number + 1, :]),
            tall(all_refs[blocks - 1 - j][number : number + 1, :]),
        )

    def across(field):
        out = {}
        for j in range(half):
            inner = [
                field[j + 1, 1 - h] if j + 1 < half else swap_block(field[j, 1 - h])
                for h in range(2)
            ]
            outer = [field[j - 1, 1 - h] if j > 0 else 0.0 for h in range(2)]
            out[j, 0] = jnp.where(low, outer[0], inner[0])
            out[j, 1] = jnp.where(low, inner[1], outer[1])
        return out

    base = ROWS * TILE_INDEX
    names = [(name, h) for name in CHUNK_FIELDS for h in range(2)]
    names += [(name, c) for name in SLOT_FIELDS for c in range(3)]
    place = {name: number for number, name in enumerate(names)}
    for j in range(half):
        found = {}
        for h in range(2):
            found["gradient", h], found["diag", h] = halves(TILE_A + h, j)
            first, second = halves(TILE_B + h, j)
            found["diag_off", h], found["vm", h] = quarters(first)
            found["cosv", h], found["sinv", h] = quarters(second)
            first, _ = halves(TILE_C + h, j)
            found["wp", h], found["wq", h] = quarters(first)
            found["g", h] = single(ROWS * (TILE_C + h) + 4, j)
            found["b", h] = single(ROWS * (TILE_C + h) + 5, j)
            found["extent", h] = single(ROWS * TILE_C + 6 + h, j)
        for c in range(3):
            found["local_main", c], found["local_off", c] = halves(TILE_LOCAL + c, j)
            found["at_from", c] = single(base + c, j)
            found["at_to", c] = single(base + 3 + c, j)
        for name, number in place.items():
            field_scr[number, j ^ mine] = found[name]

    def load(name, chunks):
        return {
            (j, c): field_scr[place[name, c], j] for j in range(half) for c in range(chunks)
        }

    def load_index(name, chunks):
        return {key: value.astype(jnp.int32) for key, value in load(name, chunks).items()}

    gradient, diag, diag_off, vm, cosv, sinv, wp, wq, g, b, extent = (
        load(name, 2) for name in CHUNK_FIELDS
    )
    vm_to, cos_to, sin_to = across(vm), across(cosv), across(sinv)
    to_diag, to_off, main, off = {}, {}, {}, {}
    for key in lane_pairs:
        h00, h01, h11, h22, h12, h02 = block_entries(
            vm[key],
            cosv[key],
            sinv[key],
            vm_to[key],
            cos_to[key],
            sin_to[key],
            g[key],
            b[key],
            wp[key],
            wq[key],
        )
        diag[key] = diag[key] + jnp.where(even, h00, h11)
        diag_off[key] = diag_off[key] + h01
        to_diag[key] = jnp.where(even, h22, h11)
        to_off[key] = -h12
        main[key] = jnp.where(even, h02, -h11)
        off[key] = jnp.where(even, -h01, h12)
    to_diag, to_off = across(to_diag), across(to_off)
    main_to = across(main)
    off_to = across({key: swap_component(off[key]) for key in lane_pairs})
    inverse, inverse_off = {}, {}
    for key in lane_pairs:
        diag[key] = diag[key] + to_diag[key]
        diag_off[key] = diag_off[key] + to_off[key]
        main[key] = main[key] + main_to[key]
        off[key] = off[key] + off_to[key]
        flipped = swap_component(diag[key])
        determinant = diag[key] * flipped - diag_off[key] * diag_off[key]
        inverse[key] = flipped / determinant
        inverse_off[key] = -diag_off[key] / determinant

    local_main, local_off = (load(name, 3) for name in SLOT_FIELDS[:2])
    at_from, at_to = (load_index(name, 3) for name in SLOT_FIELDS[2:])

    def largest(h, pairs):
        return jnp.max(functools.reduce(jnp.maximum, [extent[j, h] for j in pairs]))

    outer_rank = largest(0, [0]).astype(jnp.int32)
    inner_rank = largest(0, range(1, half)).astype(jnp.int32)
    few = (largest(1, [0]) <= 2.0 * LANES) & (largest(1, range(1, half)) <= 1.0 * LANES)

    for number in range(10):
        for s, ref in enumerate(all_refs):
            row_scr[number, s : s + 1, :] = ref[base + 6 + number : base + 7 + number, :]
    links = [row_scr[number].astype(jnp.int32) for number in range(10)]
    heads, next_f, next_t = links[:4], links[4:7], links[7:]

    def follow(rank, ends):
        for kind in range(4):
            row_scr[kind] = ends[kind].astype(jnp.float32)
            for j in range(half):
                here = tall(row_scr[kind, j : j + 1, :])
                there = tall(row_scr[kind, blocks - 1 - j : blocks - j, :])
                chain_scr[rank, kind, j ^ mine] = jnp.where(near, here, there).astype(jnp.int32)
        return tuple(
            take_chunks(next_f if kind < 2 else next_t, ends[kind]) for kind in range(4)
        )

    ends = tuple(heads)
    for rank in range(SET_RANKS_OUTER):
        ends = follow(rank, ends)
    lax.fori_loop(SET_RANKS_OUTER, jnp.maximum(outer_rank, inner_rank), follow, ends)

    def local_sums(v, sums, outer_chunks, inner_chunks):
        chunks = [outer_chunks] + [inner_chunks] * (half - 1)
        to_from, to_to = {}, {}
        for j in range(half):
            table = [v[j, 0], v[j, 1]]
            for c in range(chunks[j]):
                far = take_chunks(table, at_to[j, c])
                near = take_chunks(table, at_from[j, c])
                to_from[j, c] = local_main[j, c] * far + local_off[j, c] * swap_component(far)
                to_to[j, c] = local_main[j, c] * near + swap_component(local_off[j, c] * near)

        def add_rank(pairs, rank, sums):
            sums = list(sums)
            for number, (j, h) in enumerate(lane_pairs):
                if j in pairs:
                    for offset, terms in ((0, to_from), (2, to_to)):
                        sums[number] += take_listed(
                            [terms[j, c] for c in range(chunks[j])], chain_scr[rank, offset + h, j]
                        )
            return tuple(sums)

        for rank in range(SET_RANKS_OUTER):
            sums = add_rank(range(half if rank < SET_RANKS else 1), rank, sums)
        inner = functools.partial(add_rank, range(1, half))
        sums = lax.fori_loop(SET_RANKS, inner_rank, inner, sums)
        return lax.fori_loop(SET_RANKS_OUTER, outer_rank, functools.partial(add_rank, [0]), sums)

    def operator(v):
        flipped = {key: swap_component(v[key]) for key in lane_pairs}
        v_to, flipped_to = across(v), across(flipped)
        out = tuple(
            diag[key] * v[key]
            + diag_off[key] * flipped[key]
            + main[key] * v_to[key]
            + off[key] * flipped_to[key]
            for key in lane_pairs
        )
        sums = lax.cond(
            few, lambda: local_sums(v, out, 2, 1), lambda: local_sums(v, out, 3, 3)
        )
        return dict(zip(lane_pairs, sums))

    def scenario_total(left, right):
        total = functools.reduce(jnp.add, [left[key] * right[key] for key in lane_pairs])
        total = total + pltpu.roll(total, 2, 0)
        total = total + pltpu.roll(total, 4, 0)
        return jnp.broadcast_to(jnp.sum(total, axis=1, keepdims=True), (ROWS, LANES))

    def precondition(v):
        return {
            key: inverse[key] * v[key] + inverse_off[key] * swap_component(v[key])
            for key in lane_pairs
        }

    residual = gradient
    search = precondition(residual)
    energy = scenario_total(residual, search)
    update = None
    for iteration in range(ITERS):
        image = operator(search)
        step_size = energy / scenario_total(search, image)
        if update is None:
            update = {key: step_size * search[key] for key in lane_pairs}
        else:
            update = {key: update[key] + step_size * search[key] for key in lane_pairs}
        residual = {key: residual[key] - step_size * image[key] for key in lane_pairs}
        if iteration + 1 < ITERS:
            scaled = precondition(residual)
            energy_next = scenario_total(residual, scaled)
            ratio = energy_next / energy
            search = {key: scaled[key] + ratio * search[key] for key in lane_pairs}
            energy = energy_next

    for field, keep_scr, out_ref in (
        (update, step_scr, step_ref),
        (residual, residual_scr, residual_ref),
    ):
        for j, h in lane_pairs:
            keep_scr[j, h] = field[j, h]
        own = []
        for h in range(2):
            tile = keep_scr[mine, h]
            own.append(jnp.where(upper, swap_block(tile), tile))
        for m in range(2):
            width = min(LANES, bus_count - LANES * m)
            values = take_chunks(own, tall(pos_ref[m : m + 1, :]))
            for comp in range(2):
                out_ref[comp, :, LANES * m : LANES * m + width] = values[
                    2 * comp : 2 * comp + 2, :width
                ]


def fast_body(
    volt_mag,
    volt_ang,
    gradient,
    branch_from,
    branch_to,
    branch_count,
    boundary,
    conductance,
    susceptance,
    duals,
    slacks,
    gen_bus,
    gen_curvature,
):
    bus_count = volt_mag.shape[0]
    slot_count = branch_from.shape[0]
    blocks = lax.axis_size("net")
    vmem = pl.BlockSpec(memory_space=pltpu.VMEM)
    smem = pl.BlockSpec(memory_space=pltpu.SMEM)
    payload, position = pl.pallas_call(
        prepare_kernel,
        out_shape=(
            pltpu.VMEM((PAYLOAD_ROWS, LANES), jnp.float32),
            pltpu.VMEM((2, LANES), jnp.int32),
        ),
        in_specs=[vmem] * 13,
        out_specs=(vmem, vmem),
        scratch_shapes=[
            pltpu.VMEM((24, 2 * LANES), jnp.float32),
            pltpu.VMEM((8, 3 * LANES), jnp.float32),
            pltpu.VMEM((8, 3 * LANES), jnp.int32),
        ],
        name="prepare",
    )(
        volt_mag.T,
        volt_ang.T,
        jnp.transpose(gradient, (1, 2, 0)),
        branch_from,
        branch_to,
        branch_count,
        boundary,
        conductance,
        susceptance,
        jnp.transpose(duals, (0, 2, 1)),
        jnp.transpose(slacks, (0, 2, 1)),
        gen_bus,
        gen_curvature,
    )
    def passed(block, other):
        return lax.ppermute(block, "net", [(i, i ^ other) for i in range(blocks)])

    gathered = {0: payload}
    for other in range(2, blocks, 2):
        gathered[other] = passed(payload, other)
    for other in range(0, blocks, 2):
        gathered[other + 1] = passed(gathered[other], 1)
    gathered = [gathered[other] for other in range(blocks)]
    me = lax.axis_index("net").astype(jnp.int32)[None]
    tile_pairs = (blocks // 2, 2, ROWS, LANES)
    field = jax.ShapeDtypeStruct((2, 2, bus_count), jnp.float32)
    step, residual = pl.pallas_call(
        solve_kernel,
        out_shape=(field, field),
        in_specs=[smem] + [vmem] * (1 + blocks),
        out_specs=(vmem, vmem),
        scratch_shapes=[
            pltpu.VMEM((slot_count, 4, blocks // 2, ROWS, LANES), jnp.int32),
            pltpu.VMEM((10, blocks, LANES), jnp.float32),
            pltpu.VMEM(
                (2 * len(CHUNK_FIELDS) + 3 * len(SLOT_FIELDS), blocks // 2, ROWS, LANES),
                jnp.float32,
            ),
            pltpu.VMEM(tile_pairs, jnp.float32),
            pltpu.VMEM(tile_pairs, jnp.float32),
        ],
        compiler_params=pltpu.CompilerParams(vmem_limit_bytes=40 * 2**20),
        name="solve",
    )(me, position, *gathered)
    return jnp.transpose(step, (2, 0, 1)), jnp.transpose(residual, (2, 0, 1))


def any_body(*arrays):
    volt_mag, boundary, branch_from, gen_bus = arrays[0], arrays[6], arrays[3], arrays[11]
    fast = fits_fast_path(
        lax.axis_size("net"),
        volt_mag.shape[0],
        boundary.shape[0] // 2,
        branch_from.shape[0],
        gen_bus.shape[0],
        volt_mag.shape[1],
    )
    return fast_body(*arrays) if fast else body(*arrays)


def solution(mesh):
    placed = (
        P("net", "scen"),
        P("net", "scen"),
        P("net", None, "scen"),
        P("net"),
        P("net"),
        P("net"),
        P("net"),
        P("net"),
        P("net"),
        P(None, "net", "scen"),
        P(None, "net", "scen"),
        P("net"),
        P("net"),
    )
    return jax.shard_map(
        any_body,
        mesh=mesh,
        in_specs=placed,
        out_specs=(P("net", None, "scen"), P("net", None, "scen")),
        check_vma=False,
    )
```

profile of v0, /device:TPU:0, one launch (start us, length us, event | category | flops | bytes accessed | tf_op | source)
XLA Modules:
  0.0 22.6 jit_solution(7340554954161015430)
XLA Ops:
  1.3 1.9 %prepare.1 = (f32[88,128]{1,0:T(8,128)S(1)}, s32[2,128]{1,0:T(2,128)S(1)}) custom-call(f32[2,240]{1,0:T(2,128)} %bitcast.11, f32[2,240]{1,0:T(2,128)} %bitcast.12, f32[2,2,240]{2,1,0:T(2,128)} %bitcast.10, s32[320]{0:T(512)} %from_ref.1, s32[320]{0:T(512)} %to_ref.1, s32[1]{0:T(128)S(6)} %copy.15.count_ref, s32[240]{0:T(256)} %bound_ref.1, f32[320]{0:T(512)} %g_ref.1, ...), custom_call_target="tpu_custom_call" | custom-call | tf_op jit(solution)/shard_map/prepare/pallas_call | solution.py:801
  3.2 5.1 %collective-permute-start.5 = (f32[88,128]{1,0:T(8,128)S(1)}, f32[88,128]{1,0:T(8,128)S(1)}, u32[]{:S(2)}, u32[]{:S(2)}) collective-permute-start(f32[88,128]{1,0:T(8,128)S(1)} %get-tuple-element.7.refs_0_), channel_id=1, source_target_pairs={{0,24},{4,28},{8,16},{12,20},{16,8},{20,12},{24,0},{28,4},{1,25},{... | collective-permute-start | bytes 135176 | tf_op jit(solution)/shard_map/ppermute | solution.py:831
  8.3 0.0 collective-permute-start.3
  8.3 0.6 %collective-permute-start.1 = (f32[88,128]{1,0:T(8,128)S(1)}, f32[88,128]{1,0:T(8,128)S(1)}, u32[]{:S(2)}, u32[]{:S(2)}) collective-permute-start(f32[88,128]{1,0:T(8,128)S(1)} %get-tuple-element.7.refs_0_), channel_id=1, source_target_pairs={{0,8},{4,12},{8,0},{12,4},{16,24},{20,28},{24,16},{28,20},{1,9},{5... | collective-permute-start | bytes 135176 | tf_op jit(solution)/shard_map/ppermute | solution.py:831
  8.9 1.7 %collective-permute-start = (f32[88,128]{1,0:T(8,128)S(1)}, f32[88,128]{1,0:T(8,128)S(1)}, u32[]{:S(2)}, u32[]{:S(2)}) collective-permute-start(f32[88,128]{1,0:T(8,128)S(1)} %get-tuple-element.7.refs_0_), channel_id=1, source_target_pairs={{0,4},{4,0},{8,12},{12,8},{16,20},{20,16},{24,28},{28,24},{1,5},{5... | collective-permute-start | bytes 135176 | tf_op jit(solution)/shard_map/ppermute | solution.py:831
  10.6 0.0 collective-permute-done.5.refs_6_
  10.6 1.7 %collective-permute-start.6 = (f32[88,128]{1,0:T(8,128)S(1)}, f32[88,128]{1,0:T(8,128)S(1)}, u32[]{:S(2)}, u32[]{:S(2)}) collective-permute-start(f32[88,128]{1,0:T(8,128)S(1)} %collective-permute-done.5.refs_6_), channel_id=1, source_target_pairs={{0,4},{4,0},{8,12},{12,8},{16,20},{20,16},{24,28},{28,24},{1,5},{5... | collective-permute-start | bytes 135176 | tf_op jit(solution)/shard_map/ppermute | solution.py:831
  12.3 1.0 %collective-permute-done.3.refs_4_ = f32[88,128]{1,0:T(8,128)S(1)} collective-permute-done((f32[88,128]{1,0:T(8,128)S(1)}, f32[88,128]{1,0:T(8,128)S(1)}, u32[]{:S(2)}, u32[]{:S(2)}) %collective-permute-start.3) | collective-permute-done | bytes 45088 | tf_op jit(solution)/shard_map/ppermute | solution.py:831
  13.2 1.5 %collective-permute-start.4 = (f32[88,128]{1,0:T(8,128)S(1)}, f32[88,128]{1,0:T(8,128)S(1)}, u32[]{:S(2)}, u32[]{:S(2)}) collective-permute-start(f32[88,128]{1,0:T(8,128)S(1)} %collective-permute-done.3.refs_4_), channel_id=1, source_target_pairs={{0,4},{4,0},{8,12},{12,8},{16,20},{20,16},{24,28},{28,24},{1,5},{5... | collective-permute-start | bytes 135176 | tf_op jit(solution)/shard_map/ppermute | solution.py:831
  14.8 0.0 collective-permute-done.1.refs_2_
  14.8 0.5 %collective-permute-start.2 = (f32[88,128]{1,0:T(8,128)S(1)}, f32[88,128]{1,0:T(8,128)S(1)}, u32[]{:S(2)}, u32[]{:S(2)}) collective-permute-start(f32[88,128]{1,0:T(8,128)S(1)} %collective-permute-done.1.refs_2_), channel_id=1, source_target_pairs={{0,4},{4,0},{8,12},{12,8},{16,20},{20,16},{24,28},{28,24},{1,5},{5... | collective-permute-start | bytes 135176 | tf_op jit(solution)/shard_map/ppermute | solution.py:831
  15.3 0.0 collective-permute-done.refs_1_
  15.3 0.0 collective-permute-done.6.refs_7_
  15.3 2.0 %collective-permute-done.4.refs_5_ = f32[88,128]{1,0:T(8,128)S(1)} collective-permute-done((f32[88,128]{1,0:T(8,128)S(1)}, f32[88,128]{1,0:T(8,128)S(1)}, u32[]{:S(2)}, u32[]{:S(2)}) %collective-permute-start.4) | collective-permute-done | bytes 45088 | tf_op jit(solution)/shard_map/ppermute | solution.py:831
  17.3 1.5 %collective-permute-done.2.refs_3_ = f32[88,128]{1,0:T(8,128)S(1)} collective-permute-done((f32[88,128]{1,0:T(8,128)S(1)}, f32[88,128]{1,0:T(8,128)S(1)}, u32[]{:S(2)}, u32[]{:S(2)}) %collective-permute-start.2) | collective-permute-done | bytes 45088 | tf_op jit(solution)/shard_map/ppermute | solution.py:831
  18.8 3.8 %solve.1 = (f32[2,2,240]{2,1,0:T(2,128)}, f32[2,2,240]{2,1,0:T(2,128)}) custom-call(s32[1]{0:T(128)} %bitcast.me_ref, s32[2,128]{1,0:T(2,128)S(1)} %get-tuple-element.6.pos_ref, f32[88,128]{1,0:T(8,128)S(1)} %get-tuple-element.7.refs_0_, f32[88,128]{1,0:T(8,128)S(1)} %collective-permute-done.refs_1_, f32[88,128]{1,0:T(8,128)S(1)} %collective-permute-done.1.refs_2_, ...), custom_call_target="tpu_custom_call" | custom-call | tf_op jit(solution)/shard_map/solve/pallas_call | solution.py:842
Async XLA Ops:
  3.2 7.4 %collective-permute-start.5 = (f32[88,128]{1,0:T(8,128)S(1)}, f32[88,128]{1,0:T(8,128)S(1)}, u32[]{:S(2)}, u32[]{:S(2)}) collective-permute-start(f32[88,128]{1,0:T(8,128)S(1)} %get-tuple-element.7.refs_0_), channel_id=1, source_target_pairs={{0,24},{4,28},{8,16},{12,20},{16,8},{20,12},{24,0},{28,4},{1,25},{... | collective-permute-start | bytes 135176 | tf_op jit(solution)/shard_map/ppermute | solution.py:831
  8.3 4.9 %collective-permute-start.3 = (f32[88,128]{1,0:T(8,128)S(1)}, f32[88,128]{1,0:T(8,128)S(1)}, u32[]{:S(2)}, u32[]{:S(2)}) collective-permute-start(f32[88,128]{1,0:T(8,128)S(1)} %get-tuple-element.7.refs_0_), channel_id=1, source_target_pairs={{0,16},{4,20},{8,24},{12,28},{16,0},{20,4},{24,8},{28,12},{1,17},{... | collective-permute-start | bytes 135176 | tf_op jit(solution)/shard_map/ppermute | solution.py:831
  8.3 6.5 %collective-permute-start.1 = (f32[88,128]{1,0:T(8,128)S(1)}, f32[88,128]{1,0:T(8,128)S(1)}, u32[]{:S(2)}, u32[]{:S(2)}) collective-permute-start(f32[88,128]{1,0:T(8,128)S(1)} %get-tuple-element.7.refs_0_), channel_id=1, source_target_pairs={{0,8},{4,12},{8,0},{12,4},{16,24},{20,28},{24,16},{28,20},{1,9},{5... | collective-permute-start | bytes 135176 | tf_op jit(solution)/shard_map/ppermute | solution.py:831
  8.9 6.3 %collective-permute-start = (f32[88,128]{1,0:T(8,128)S(1)}, f32[88,128]{1,0:T(8,128)S(1)}, u32[]{:S(2)}, u32[]{:S(2)}) collective-permute-start(f32[88,128]{1,0:T(8,128)S(1)} %get-tuple-element.7.refs_0_), channel_id=1, source_target_pairs={{0,4},{4,0},{8,12},{12,8},{16,20},{20,16},{24,28},{28,24},{1,5},{5... | collective-permute-start | bytes 135176 | tf_op jit(solution)/shard_map/ppermute | solution.py:831
  10.6 4.7 %collective-permute-start.6 = (f32[88,128]{1,0:T(8,128)S(1)}, f32[88,128]{1,0:T(8,128)S(1)}, u32[]{:S(2)}, u32[]{:S(2)}) collective-permute-start(f32[88,128]{1,0:T(8,128)S(1)} %collective-permute-done.5.refs_6_), channel_id=1, source_target_pairs={{0,4},{4,0},{8,12},{12,8},{16,20},{20,16},{24,28},{28,24},{1,5},{5... | collective-permute-start | bytes 135176 | tf_op jit(solution)/shard_map/ppermute | solution.py:831
  13.2 4.0 %collective-permute-start.4 = (f32[88,128]{1,0:T(8,128)S(1)}, f32[88,128]{1,0:T(8,128)S(1)}, u32[]{:S(2)}, u32[]{:S(2)}) collective-permute-start(f32[88,128]{1,0:T(8,128)S(1)} %collective-permute-done.3.refs_4_), channel_id=1, source_target_pairs={{0,4},{4,0},{8,12},{12,8},{16,20},{20,16},{24,28},{28,24},{1,5},{5... | collective-permute-start | bytes 135176 | tf_op jit(solution)/shard_map/ppermute | solution.py:831
  14.8 4.0 %collective-permute-start.2 = (f32[88,128]{1,0:T(8,128)S(1)}, f32[88,128]{1,0:T(8,128)S(1)}, u32[]{:S(2)}, u32[]{:S(2)}) collective-permute-start(f32[88,128]{1,0:T(8,128)S(1)} %collective-permute-done.1.refs_2_), channel_id=1, source_target_pairs={{0,4},{4,0},{8,12},{12,8},{16,20},{20,16},{24,28},{28,24},{1,5},{5... | collective-permute-start | bytes 135176 | tf_op jit(solution)/shard_map/ppermute | solution.py:831
where the time goes:
time: 22.8 us; the launch traced here: 22.6 us
  starting transfers between devices  11.1 us (49%)
  Pallas kernels  5.68 us (25%)
  waiting for transfers between devices  4.52 us (20%)
  between operations  1.29 us (6%)
    ppermute x7, starting transfers between devices, passed(): return lax.ppermute(block, 'net', [(i, i ^ other) for i in range(blocks)])  11.1 us
    ppermute x7, waiting for transfers between devices, passed(): return lax.ppermute(block, 'net', [(i, i ^ other) for i in range(blocks)])  4.52 us
    pallas_call x1, Pallas kernels, fast_body(): pl.pallas_call(solve_kernel, out_shape=(field, field), in_specs=[smem] +...  3.78 us
    pallas_call x1, Pallas kernels, fast_body(): pl.pallas_call(prepare_kernel, out_shape=(pltpu.VMEM((PAYLOAD_ROWS, LANES...  1.91 us
  transfers between devices with their start and end apart: 7, of which 3 were waited for; matrix products, arithmetic and copies ran while one was open for 0% of the time, Pallas kernels for 0%

commit v1 on v0

--- a/solution.py
+++ b/solution.py
@@ -228,7 +228,7 @@
 CHUNK_FIELDS += ["wp", "wq", "g", "b", "extent"]
 SLOT_FIELDS = ["local_main", "local_off", "at_from", "at_to"]
 SET_RANKS = 4
-SET_RANKS_OUTER = 6
+SET_RANKS_OUTER = 4
 
 
 def fits_fast_path(blocks, bus_count, ghost_count, slot_count, gen_count, scen_count):
@@ -530,7 +530,8 @@
 
 
 def solve_kernel(me_ref, pos_ref, *refs):
-    *all_refs, step_ref, residual_ref, chain_scr, row_scr, field_scr, step_scr, residual_scr = refs
+    *all_refs, step_ref, residual_ref = refs[:-6]
+    chain_scr, end_scr, row_scr, field_scr, step_scr, residual_scr = refs[-6:]
     blocks = len(all_refs)
     me = me_ref[0]
     half = blocks // 2
@@ -672,11 +673,11 @@
 
     def follow(rank, ends):
         for kind in range(4):
-            row_scr[kind] = ends[kind].astype(jnp.float32)
+            end_scr[rank, kind] = ends[kind]
             for j in range(half):
-                here = tall(row_scr[kind, j : j + 1, :])
-                there = tall(row_scr[kind, blocks - 1 - j : blocks - j, :])
-                chain_scr[rank, kind, j ^ mine] = jnp.where(near, here, there).astype(jnp.int32)
+                here = tall(end_scr[rank, kind, j : j + 1, :])
+                there = tall(end_scr[rank, kind, blocks - 1 - j : blocks - j, :])
+                chain_scr[rank, kind, j ^ mine] = jnp.where(near, here, there)
         return tuple(
             take_chunks(next_f if kind < 2 else next_t, ends[kind]) for kind in range(4)
         )
@@ -846,6 +847,7 @@
         out_specs=(vmem, vmem),
         scratch_shapes=[
             pltpu.VMEM((slot_count, 4, blocks // 2, ROWS, LANES), jnp.int32),
+            pltpu.VMEM((slot_count, 4, blocks, LANES), jnp.int32),
             pltpu.VMEM((10, blocks, LANES), jnp.float32),
             pltpu.VMEM(
                 (2 * len(CHUNK_FIELDS) + 3 * len(SLOT_FIELDS), blocks // 2, ROWS, LANES),

time: 22.8 us -> 22.4 us (0.982)
  Pallas kernels: 5.68 us -> 5.33 us
    pallas_call x1, Pallas kernels: 3.78 us -> 3.42 us  [fast_body(): pl.pallas_call(solve_kernel, out_shape=(field, field), in_specs=[smem] +...]
where the time goes in v1:
time: 22.4 us; the launch traced here: 22.2 us
  starting transfers between devices  11.1 us (50%)
  Pallas kernels  5.33 us (24%)
  waiting for transfers between devices  4.52 us (20%)
  between operations  1.29 us (6%)
    ppermute x7, starting transfers between devices, passed(): return lax.ppermute(block, 'net', [(i, i ^ other) for i in range(blocks)])  11.1 us
    ppermute x7, waiting for transfers between devices, passed(): return lax.ppermute(block, 'net', [(i, i ^ other) for i in range(blocks)])  4.52 us
    pallas_call x1, Pallas kernels, fast_body(): pl.pallas_call(solve_kernel, out_shape=(field, field), in_specs=[smem] +...  3.42 us
    pallas_call x1, Pallas kernels, fast_body(): pl.pallas_call(prepare_kernel, out_shape=(pltpu.VMEM((PAYLOAD_ROWS, LANES...  1.91 us
  transfers between devices with their start and end apart: 7, of which 3 were waited for; matrix products, arithmetic and copies ran while one was open for 0% of the time, Pallas kernels for 0%

profile of v1, /device:TPU:0, one launch (start us, length us, event | category | flops | bytes accessed | tf_op | source)
XLA Modules:
  0.0 22.2 jit_solution(15767147077453535949)
XLA Ops:
  1.3 1.9 %prepare.1 = (f32[88,128]{1,0:T(8,128)S(1)}, s32[2,128]{1,0:T(2,128)S(1)}) custom-call(f32[2,240]{1,0:T(2,128)} %bitcast.11, f32[2,240]{1,0:T(2,128)} %bitcast.12, f32[2,2,240]{2,1,0:T(2,128)} %bitcast.10, s32[320]{0:T(512)} %from_ref.1, s32[320]{0:T(512)} %to_ref.1, s32[1]{0:T(128)S(6)} %copy.15.count_ref, s32[240]{0:T(256)} %bound_ref.1, f32[320]{0:T(512)} %g_ref.1, ...), custom_call_target="tpu_custom_call" | custom-call | tf_op jit(solution)/shard_map/prepare/pallas_call | solution.py:802
  3.2 5.1 %collective-permute-start.5 = (f32[88,128]{1,0:T(8,128)S(1)}, f32[88,128]{1,0:T(8,128)S(1)}, u32[]{:S(2)}, u32[]{:S(2)}) collective-permute-start(f32[88,128]{1,0:T(8,128)S(1)} %get-tuple-element.7.refs_0_), channel_id=1, source_target_pairs={{0,24},{4,28},{8,16},{12,20},{16,8},{20,12},{24,0},{28,4},{1,25},{... | collective-permute-start | bytes 135176 | tf_op jit(solution)/shard_map/ppermute | solution.py:832
  8.3 0.0 collective-permute-start.3
  8.3 0.6 %collective-permute-start.1 = (f32[88,128]{1,0:T(8,128)S(1)}, f32[88,128]{1,0:T(8,128)S(1)}, u32[]{:S(2)}, u32[]{:S(2)}) collective-permute-start(f32[88,128]{1,0:T(8,128)S(1)} %get-tuple-element.7.refs_0_), channel_id=1, source_target_pairs={{0,8},{4,12},{8,0},{12,4},{16,24},{20,28},{24,16},{28,20},{1,9},{5... | collective-permute-start | bytes 135176 | tf_op jit(solution)/shard_map/ppermute | solution.py:832
  8.9 1.7 %collective-permute-start = (f32[88,128]{1,0:T(8,128)S(1)}, f32[88,128]{1,0:T(8,128)S(1)}, u32[]{:S(2)}, u32[]{:S(2)}) collective-permute-start(f32[88,128]{1,0:T(8,128)S(1)} %get-tuple-element.7.refs_0_), channel_id=1, source_target_pairs={{0,4},{4,0},{8,12},{12,8},{16,20},{20,16},{24,28},{28,24},{1,5},{5... | collective-permute-start | bytes 135176 | tf_op jit(solution)/shard_map/ppermute | solution.py:832
  10.6 0.0 collective-permute-done.5.refs_6_
  10.6 1.7 %collective-permute-start.6 = (f32[88,128]{1,0:T(8,128)S(1)}, f32[88,128]{1,0:T(8,128)S(1)}, u32[]{:S(2)}, u32[]{:S(2)}) collective-permute-start(f32[88,128]{1,0:T(8,128)S(1)} %collective-permute-done.5.refs_6_), channel_id=1, source_target_pairs={{0,4},{4,0},{8,12},{12,8},{16,20},{20,16},{24,28},{28,24},{1,5},{5... | collective-permute-start | bytes 135176 | tf_op jit(solution)/shard_map/ppermute | solution.py:832
  12.3 1.0 %collective-permute-done.3.refs_4_ = f32[88,128]{1,0:T(8,128)S(1)} collective-permute-done((f32[88,128]{1,0:T(8,128)S(1)}, f32[88,128]{1,0:T(8,128)S(1)}, u32[]{:S(2)}, u32[]{:S(2)}) %collective-permute-start.3) | collective-permute-done | bytes 45088 | tf_op jit(solution)/shard_map/ppermute | solution.py:832
  13.2 1.5 %collective-permute-start.4 = (f32[88,128]{1,0:T(8,128)S(1)}, f32[88,128]{1,0:T(8,128)S(1)}, u32[]{:S(2)}, u32[]{:S(2)}) collective-permute-start(f32[88,128]{1,0:T(8,128)S(1)} %collective-permute-done.3.refs_4_), channel_id=1, source_target_pairs={{0,4},{4,0},{8,12},{12,8},{16,20},{20,16},{24,28},{28,24},{1,5},{5... | collective-permute-start | bytes 135176 | tf_op jit(solution)/shard_map/ppermute | solution.py:832
  14.8 0.0 collective-permute-done.1.refs_2_
  14.8 0.5 %collective-permute-start.2 = (f32[88,128]{1,0:T(8,128)S(1)}, f32[88,128]{1,0:T(8,128)S(1)}, u32[]{:S(2)}, u32[]{:S(2)}) collective-permute-start(f32[88,128]{1,0:T(8,128)S(1)} %collective-permute-done.1.refs_2_), channel_id=1, source_target_pairs={{0,4},{4,0},{8,12},{12,8},{16,20},{20,16},{24,28},{28,24},{1,5},{5... | collective-permute-start | bytes 135176 | tf_op jit(solution)/shard_map/ppermute | solution.py:832
  15.3 0.0 collective-permute-done.refs_1_
  15.3 0.0 collective-permute-done.6.refs_7_
  15.3 2.0 %collective-permute-done.4.refs_5_ = f32[88,128]{1,0:T(8,128)S(1)} collective-permute-done((f32[88,128]{1,0:T(8,128)S(1)}, f32[88,128]{1,0:T(8,128)S(1)}, u32[]{:S(2)}, u32[]{:S(2)}) %collective-permute-start.4) | collective-permute-done | bytes 45088 | tf_op jit(solution)/shard_map/ppermute | solution.py:832
  17.3 1.5 %collective-permute-done.2.refs_3_ = f32[88,128]{1,0:T(8,128)S(1)} collective-permute-done((f32[88,128]{1,0:T(8,128)S(1)}, f32[88,128]{1,0:T(8,128)S(1)}, u32[]{:S(2)}, u32[]{:S(2)}) %collective-permute-start.2) | collective-permute-done | bytes 45088 | tf_op jit(solution)/shard_map/ppermute | solution.py:832
  18.8 3.4 %solve.1 = (f32[2,2,240]{2,1,0:T(2,128)}, f32[2,2,240]{2,1,0:T(2,128)}) custom-call(s32[1]{0:T(128)} %bitcast.me_ref, s32[2,128]{1,0:T(2,128)S(1)} %get-tuple-element.6.pos_ref, f32[88,128]{1,0:T(8,128)S(1)} %get-tuple-element.7.refs_0_, f32[88,128]{1,0:T(8,128)S(1)} %collective-permute-done.refs_1_, f32[88,128]{1,0:T(8,128)S(1)} %collective-permute-done.1.refs_2_, ...), custom_call_target="tpu_custom_call" | custom-call | tf_op jit(solution)/shard_map/solve/pallas_call | solution.py:843
Async XLA Ops:
  3.2 7.4 %collective-permute-start.5 = (f32[88,128]{1,0:T(8,128)S(1)}, f32[88,128]{1,0:T(8,128)S(1)}, u32[]{:S(2)}, u32[]{:S(2)}) collective-permute-start(f32[88,128]{1,0:T(8,128)S(1)} %get-tuple-element.7.refs_0_), channel_id=1, source_target_pairs={{0,24},{4,28},{8,16},{12,20},{16,8},{20,12},{24,0},{28,4},{1,25},{... | collective-permute-start | bytes 135176 | tf_op jit(solution)/shard_map/ppermute | solution.py:832
  8.3 4.9 %collective-permute-start.3 = (f32[88,128]{1,0:T(8,128)S(1)}, f32[88,128]{1,0:T(8,128)S(1)}, u32[]{:S(2)}, u32[]{:S(2)}) collective-permute-start(f32[88,128]{1,0:T(8,128)S(1)} %get-tuple-element.7.refs_0_), channel_id=1, source_target_pairs={{0,16},{4,20},{8,24},{12,28},{16,0},{20,4},{24,8},{28,12},{1,17},{... | collective-permute-start | bytes 135176 | tf_op jit(solution)/shard_map/ppermute | solution.py:832
  8.3 6.5 %collective-permute-start.1 = (f32[88,128]{1,0:T(8,128)S(1)}, f32[88,128]{1,0:T(8,128)S(1)}, u32[]{:S(2)}, u32[]{:S(2)}) collective-permute-start(f32[88,128]{1,0:T(8,128)S(1)} %get-tuple-element.7.refs_0_), channel_id=1, source_target_pairs={{0,8},{4,12},{8,0},{12,4},{16,24},{20,28},{24,16},{28,20},{1,9},{5... | collective-permute-start | bytes 135176 | tf_op jit(solution)/shard_map/ppermute | solution.py:832
  8.9 6.3 %collective-permute-start = (f32[88,128]{1,0:T(8,128)S(1)}, f32[88,128]{1,0:T(8,128)S(1)}, u32[]{:S(2)}, u32[]{:S(2)}) collective-permute-start(f32[88,128]{1,0:T(8,128)S(1)} %get-tuple-element.7.refs_0_), channel_id=1, source_target_pairs={{0,4},{4,0},{8,12},{12,8},{16,20},{20,16},{24,28},{28,24},{1,5},{5... | collective-permute-start | bytes 135176 | tf_op jit(solution)/shard_map/ppermute | solution.py:832
  10.6 4.7 %collective-permute-start.6 = (f32[88,128]{1,0:T(8,128)S(1)}, f32[88,128]{1,0:T(8,128)S(1)}, u32[]{:S(2)}, u32[]{:S(2)}) collective-permute-start(f32[88,128]{1,0:T(8,128)S(1)} %collective-permute-done.5.refs_6_), channel_id=1, source_target_pairs={{0,4},{4,0},{8,12},{12,8},{16,20},{20,16},{24,28},{28,24},{1,5},{5... | collective-permute-start | bytes 135176 | tf_op jit(solution)/shard_map/ppermute | solution.py:832
  13.2 4.0 %collective-permute-start.4 = (f32[88,128]{1,0:T(8,128)S(1)}, f32[88,128]{1,0:T(8,128)S(1)}, u32[]{:S(2)}, u32[]{:S(2)}) collective-permute-start(f32[88,128]{1,0:T(8,128)S(1)} %collective-permute-done.3.refs_4_), channel_id=1, source_target_pairs={{0,4},{4,0},{8,12},{12,8},{16,20},{20,16},{24,28},{28,24},{1,5},{5... | collective-permute-start | bytes 135176 | tf_op jit(solution)/shard_map/ppermute | solution.py:832
  14.8 4.0 %collective-permute-start.2 = (f32[88,128]{1,0:T(8,128)S(1)}, f32[88,128]{1,0:T(8,128)S(1)}, u32[]{:S(2)}, u32[]{:S(2)}) collective-permute-start(f32[88,128]{1,0:T(8,128)S(1)} %collective-permute-done.1.refs_2_), channel_id=1, source_target_pairs={{0,4},{4,0},{8,12},{12,8},{16,20},{20,16},{24,28},{28,24},{1,5},{5... | collective-permute-start | bytes 135176 | tf_op jit(solution)/shard_map/ppermute | solution.py:832

commit v2 on v1

--- a/solution.py
+++ b/solution.py
@@ -614,9 +614,6 @@
             (j, c): field_scr[place[name, c], j] for j in range(half) for c in range(chunks)
         }
 
-    def load_index(name, chunks):
-        return {key: value.astype(jnp.int32) for key, value in load(name, chunks).items()}
-
     gradient, diag, diag_off, vm, cosv, sinv, wp, wq, g, b, extent = (
         load(name, 2) for name in CHUNK_FIELDS
     )
@@ -655,9 +652,6 @@
         inverse[key] = flipped / determinant
         inverse_off[key] = -diag_off[key] / determinant
 
-    local_main, local_off = (load(name, 3) for name in SLOT_FIELDS[:2])
-    at_from, at_to = (load_index(name, 3) for name in SLOT_FIELDS[2:])
-
     def largest(h, pairs):
         return jnp.max(functools.reduce(jnp.maximum, [extent[j, h] for j in pairs]))
 
@@ -693,10 +687,13 @@
         for j in range(half):
             table = [v[j, 0], v[j, 1]]
             for c in range(chunks[j]):
-                far = take_chunks(table, at_to[j, c])
-                near = take_chunks(table, at_from[j, c])
-                to_from[j, c] = local_main[j, c] * far + local_off[j, c] * swap_component(far)
-                to_to[j, c] = local_main[j, c] * near + swap_component(local_off[j, c] * near)
+                main_c, off_c, at_from, at_to = (
+                    field_scr[place[name, c], j] for name in SLOT_FIELDS
+                )
+                far = take_chunks(table, at_to.astype(jnp.int32))
+                near = take_chunks(table, at_from.astype(jnp.int32))
+                to_from[j, c] = main_c * far + off_c * swap_component(far)
+                to_to[j, c] = main_c * near + swap_component(off_c * near)
 
         def add_rank(pairs, rank, sums):
             sums = list(sums)

time: 22.4 us -> 22.6 us (level); the launches traced: 22.2 us -> 22.7 us
  Pallas kernels: 5.33 us -> 5.78 us
    pallas_call x1, Pallas kernels: 3.42 us -> 3.88 us  [fast_body(): pl.pallas_call(solve_kernel, out_shape=(field, field), in_specs=[smem] +...]
where the time goes in v2:
time: 22.6 us; the launch traced here: 22.7 us
  starting transfers between devices  11.1 us (49%)
  Pallas kernels  5.78 us (26%)
  waiting for transfers between devices  4.52 us (20%)
  between operations  1.29 us (6%)
    ppermute x7, starting transfers between devices, passed(): return lax.ppermute(block, 'net', [(i, i ^ other) for i in range(blocks)])  11.1 us
    ppermute x7, waiting for transfers between devices, passed(): return lax.ppermute(block, 'net', [(i, i ^ other) for i in range(blocks)])  4.52 us
    pallas_call x1, Pallas kernels, fast_body(): pl.pallas_call(solve_kernel, out_shape=(field, field), in_specs=[smem] +...  3.88 us
    pallas_call x1, Pallas kernels, fast_body(): pl.pallas_call(prepare_kernel, out_shape=(pltpu.VMEM((PAYLOAD_ROWS, LANES...  1.91 us
  transfers between devices with their start and end apart: 7, of which 3 were waited for; matrix products, arithmetic and copies ran while one was open for 0% of the time, Pallas kernels for 0%

profile of v2, /device:TPU:0, one launch (start us, length us, event | category | flops | bytes accessed | tf_op | source)
XLA Modules:
  0.0 22.7 jit_solution(13199593620853150043)
XLA Ops:
  1.3 1.9 %prepare.1 = (f32[88,128]{1,0:T(8,128)S(1)}, s32[2,128]{1,0:T(2,128)S(1)}) custom-call(f32[2,240]{1,0:T(2,128)} %bitcast.11, f32[2,240]{1,0:T(2,128)} %bitcast.12, f32[2,2,240]{2,1,0:T(2,128)} %bitcast.10, s32[320]{0:T(512)} %from_ref.1, s32[320]{0:T(512)} %to_ref.1, s32[1]{0:T(128)S(6)} %copy.15.count_ref, s32[240]{0:T(256)} %bound_ref.1, f32[320]{0:T(512)} %g_ref.1, ...), custom_call_target="tpu_custom_call" | custom-call | tf_op jit(solution)/shard_map/prepare/pallas_call | solution.py:799
  3.2 5.1 %collective-permute-start.5 = (f32[88,128]{1,0:T(8,128)S(1)}, f32[88,128]{1,0:T(8,128)S(1)}, u32[]{:S(2)}, u32[]{:S(2)}) collective-permute-start(f32[88,128]{1,0:T(8,128)S(1)} %get-tuple-element.7.refs_0_), channel_id=1, source_target_pairs={{0,24},{4,28},{8,16},{12,20},{16,8},{20,12},{24,0},{28,4},{1,25},{... | collective-permute-start | bytes 135176 | tf_op jit(solution)/shard_map/ppermute | solution.py:829
  8.3 0.0 collective-permute-start.3
  8.3 0.6 %collective-permute-start.1 = (f32[88,128]{1,0:T(8,128)S(1)}, f32[88,128]{1,0:T(8,128)S(1)}, u32[]{:S(2)}, u32[]{:S(2)}) collective-permute-start(f32[88,128]{1,0:T(8,128)S(1)} %get-tuple-element.7.refs_0_), channel_id=1, source_target_pairs={{0,8},{4,12},{8,0},{12,4},{16,24},{20,28},{24,16},{28,20},{1,9},{5... | collective-permute-start | bytes 135176 | tf_op jit(solution)/shard_map/ppermute | solution.py:829
  8.9 1.7 %collective-permute-start = (f32[88,128]{1,0:T(8,128)S(1)}, f32[88,128]{1,0:T(8,128)S(1)}, u32[]{:S(2)}, u32[]{:S(2)}) collective-permute-start(f32[88,128]{1,0:T(8,128)S(1)} %get-tuple-element.7.refs_0_), channel_id=1, source_target_pairs={{0,4},{4,0},{8,12},{12,8},{16,20},{20,16},{24,28},{28,24},{1,5},{5... | collective-permute-start | bytes 135176 | tf_op jit(solution)/shard_map/ppermute | solution.py:829
  10.6 0.0 collective-permute-done.5.refs_6_
  10.6 1.7 %collective-permute-start.6 = (f32[88,128]{1,0:T(8,128)S(1)}, f32[88,128]{1,0:T(8,128)S(1)}, u32[]{:S(2)}, u32[]{:S(2)}) collective-permute-start(f32[88,128]{1,0:T(8,128)S(1)} %collective-permute-done.5.refs_6_), channel_id=1, source_target_pairs={{0,4},{4,0},{8,12},{12,8},{16,20},{20,16},{24,28},{28,24},{1,5},{5... | collective-permute-start | bytes 135176 | tf_op jit(solution)/shard_map/ppermute | solution.py:829
  12.3 1.0 %collective-permute-done.3.refs_4_ = f32[88,128]{1,0:T(8,128)S(1)} collective-permute-done((f32[88,128]{1,0:T(8,128)S(1)}, f32[88,128]{1,0:T(8,128)S(1)}, u32[]{:S(2)}, u32[]{:S(2)}) %collective-permute-start.3) | collective-permute-done | bytes 45088 | tf_op jit(solution)/shard_map/ppermute | solution.py:829
  13.2 1.5 %collective-permute-start.4 = (f32[88,128]{1,0:T(8,128)S(1)}, f32[88,128]{1,0:T(8,128)S(1)}, u32[]{:S(2)}, u32[]{:S(2)}) collective-permute-start(f32[88,128]{1,0:T(8,128)S(1)} %collective-permute-done.3.refs_4_), channel_id=1, source_target_pairs={{0,4},{4,0},{8,12},{12,8},{16,20},{20,16},{24,28},{28,24},{1,5},{5... | collective-permute-start | bytes 135176 | tf_op jit(solution)/shard_map/ppermute | solution.py:829
  14.8 0.0 collective-permute-done.1.refs_2_
  14.8 0.5 %collective-permute-start.2 = (f32[88,128]{1,0:T(8,128)S(1)}, f32[88,128]{1,0:T(8,128)S(1)}, u32[]{:S(2)}, u32[]{:S(2)}) collective-permute-start(f32[88,128]{1,0:T(8,128)S(1)} %collective-permute-done.1.refs_2_), channel_id=1, source_target_pairs={{0,4},{4,0},{8,12},{12,8},{16,20},{20,16},{24,28},{28,24},{1,5},{5... | collective-permute-start | bytes 135176 | tf_op jit(solution)/shard_map/ppermute | solution.py:829
  15.3 0.0 collective-permute-done.refs_1_
  15.3 0.0 collective-permute-done.6.refs_7_
  15.3 2.0 %collective-permute-done.4.refs_5_ = f32[88,128]{1,0:T(8,128)S(1)} collective-permute-done((f32[88,128]{1,0:T(8,128)S(1)}, f32[88,128]{1,0:T(8,128)S(1)}, u32[]{:S(2)}, u32[]{:S(2)}) %collective-permute-start.4) | collective-permute-done | bytes 45088 | tf_op jit(solution)/shard_map/ppermute | solution.py:829
  17.3 1.5 %collective-permute-done.2.refs_3_ = f32[88,128]{1,0:T(8,128)S(1)} collective-permute-done((f32[88,128]{1,0:T(8,128)S(1)}, f32[88,128]{1,0:T(8,128)S(1)}, u32[]{:S(2)}, u32[]{:S(2)}) %collective-permute-start.2) | collective-permute-done | bytes 45088 | tf_op jit(solution)/shard_map/ppermute | solution.py:829
  18.8 3.9 %solve.1 = (f32[2,2,240]{2,1,0:T(2,128)}, f32[2,2,240]{2,1,0:T(2,128)}) custom-call(s32[1]{0:T(128)} %bitcast.me_ref, s32[2,128]{1,0:T(2,128)S(1)} %get-tuple-element.6.pos_ref, f32[88,128]{1,0:T(8,128)S(1)} %get-tuple-element.7.refs_0_, f32[88,128]{1,0:T(8,128)S(1)} %collective-permute-done.refs_1_, f32[88,128]{1,0:T(8,128)S(1)} %collective-permute-done.1.refs_2_, ...), custom_call_target="tpu_custom_call" | custom-call | tf_op jit(solution)/shard_map/solve/pallas_call | solution.py:840
Async XLA Ops:
  3.2 7.4 %collective-permute-start.5 = (f32[88,128]{1,0:T(8,128)S(1)}, f32[88,128]{1,0:T(8,128)S(1)}, u32[]{:S(2)}, u32[]{:S(2)}) collective-permute-start(f32[88,128]{1,0:T(8,128)S(1)} %get-tuple-element.7.refs_0_), channel_id=1, source_target_pairs={{0,24},{4,28},{8,16},{12,20},{16,8},{20,12},{24,0},{28,4},{1,25},{... | collective-permute-start | bytes 135176 | tf_op jit(solution)/shard_map/ppermute | solution.py:829
  8.3 4.9 %collective-permute-start.3 = (f32[88,128]{1,0:T(8,128)S(1)}, f32[88,128]{1,0:T(8,128)S(1)}, u32[]{:S(2)}, u32[]{:S(2)}) collective-permute-start(f32[88,128]{1,0:T(8,128)S(1)} %get-tuple-element.7.refs_0_), channel_id=1, source_target_pairs={{0,16},{4,20},{8,24},{12,28},{16,0},{20,4},{24,8},{28,12},{1,17},{... | collective-permute-start | bytes 135176 | tf_op jit(solution)/shard_map/ppermute | solution.py:829
  8.3 6.5 %collective-permute-start.1 = (f32[88,128]{1,0:T(8,128)S(1)}, f32[88,128]{1,0:T(8,128)S(1)}, u32[]{:S(2)}, u32[]{:S(2)}) collective-permute-start(f32[88,128]{1,0:T(8,128)S(1)} %get-tuple-element.7.refs_0_), channel_id=1, source_target_pairs={{0,8},{4,12},{8,0},{12,4},{16,24},{20,28},{24,16},{28,20},{1,9},{5... | collective-permute-start | bytes 135176 | tf_op jit(solution)/shard_map/ppermute | solution.py:829
  8.9 6.3 %collective-permute-start = (f32[88,128]{1,0:T(8,128)S(1)}, f32[88,128]{1,0:T(8,128)S(1)}, u32[]{:S(2)}, u32[]{:S(2)}) collective-permute-start(f32[88,128]{1,0:T(8,128)S(1)} %get-tuple-element.7.refs_0_), channel_id=1, source_target_pairs={{0,4},{4,0},{8,12},{12,8},{16,20},{20,16},{24,28},{28,24},{1,5},{5... | collective-permute-start | bytes 135176 | tf_op jit(solution)/shard_map/ppermute | solution.py:829
  10.6 4.7 %collective-permute-start.6 = (f32[88,128]{1,0:T(8,128)S(1)}, f32[88,128]{1,0:T(8,128)S(1)}, u32[]{:S(2)}, u32[]{:S(2)}) collective-permute-start(f32[88,128]{1,0:T(8,128)S(1)} %collective-permute-done.5.refs_6_), channel_id=1, source_target_pairs={{0,4},{4,0},{8,12},{12,8},{16,20},{20,16},{24,28},{28,24},{1,5},{5... | collective-permute-start | bytes 135176 | tf_op jit(solution)/shard_map/ppermute | solution.py:829
  13.2 4.0 %collective-permute-start.4 = (f32[88,128]{1,0:T(8,128)S(1)}, f32[88,128]{1,0:T(8,128)S(1)}, u32[]{:S(2)}, u32[]{:S(2)}) collective-permute-start(f32[88,128]{1,0:T(8,128)S(1)} %collective-permute-done.3.refs_4_), channel_id=1, source_target_pairs={{0,4},{4,0},{8,12},{12,8},{16,20},{20,16},{24,28},{28,24},{1,5},{5... | collective-permute-start | bytes 135176 | tf_op jit(solution)/shard_map/ppermute | solution.py:829
  14.8 4.0 %collective-permute-start.2 = (f32[88,128]{1,0:T(8,128)S(1)}, f32[88,128]{1,0:T(8,128)S(1)}, u32[]{:S(2)}, u32[]{:S(2)}) collective-permute-start(f32[88,128]{1,0:T(8,128)S(1)} %collective-permute-done.1.refs_2_), channel_id=1, source_target_pairs={{0,4},{4,0},{8,12},{12,8},{16,20},{20,16},{24,28},{28,24},{1,5},{5... | collective-permute-start | bytes 135176 | tf_op jit(solution)/shard_map/ppermute | solution.py:829

commit v3 on v1

--- a/solution.py
+++ b/solution.py
@@ -831,11 +831,9 @@
     def passed(block, other):
         return lax.ppermute(block, "net", [(i, i ^ other) for i in range(blocks)])
 
-    gathered = {0: payload}
-    for other in range(2, blocks, 2):
-        gathered[other] = passed(payload, other)
-    for other in range(0, blocks, 2):
-        gathered[other + 1] = passed(gathered[other], 1)
+    gathered = {0: payload, 1: passed(payload, 1)}
+    for other in range(2, blocks):
+        gathered[other] = passed(gathered[other % 2], other - other % 2)
     gathered = [gathered[other] for other in range(blocks)]
     me = lax.axis_index("net").astype(jnp.int32)[None]
     tile_pairs = (blocks // 2, 2, ROWS, LANES)

time: 22.4 us -> 22.8 us (1.018)
  starting transfers between devices: 11.1 us -> 11.8 us
  waiting for transfers between devices: 4.52 us -> 4.16 us
    ppermute x7, starting transfers between devices: 11.1 us -> 11.8 us  [passed(): return lax.ppermute(block, 'net', [(i, i ^ other) for i in range(blocks)])]
    ppermute x7, waiting for transfers between devices: 4.52 us -> 4.16 us  [passed(): return lax.ppermute(block, 'net', [(i, i ^ other) for i in range(blocks)])]
where the time goes in v3:
time: 22.8 us; the launch traced here: 22.6 us
  starting transfers between devices  11.8 us (52%)
  Pallas kernels  5.33 us (23%)
  waiting for transfers between devices  4.16 us (18%)
  between operations  1.29 us (6%)
    ppermute x7, starting transfers between devices, passed(): return lax.ppermute(block, 'net', [(i, i ^ other) for i in range(blocks)])  11.8 us
    ppermute x7, waiting for transfers between devices, passed(): return lax.ppermute(block, 'net', [(i, i ^ other) for i in range(blocks)])  4.16 us
    pallas_call x1, Pallas kernels, fast_body(): pl.pallas_call(solve_kernel, out_shape=(field, field), in_specs=[smem] +...  3.42 us
    pallas_call x1, Pallas kernels, fast_body(): pl.pallas_call(prepare_kernel, out_shape=(pltpu.VMEM((PAYLOAD_ROWS, LANES...  1.91 us
  transfers between devices with their start and end apart: 7, of which 3 were waited for; matrix products, arithmetic and copies ran while one was open for 0% of the time, Pallas kernels for 0%

profile of v3, /device:TPU:0, one launch (start us, length us, event | category | flops | bytes accessed | tf_op | source)
XLA Modules:
  0.0 22.6 jit_solution(12361957559585890185)
XLA Ops:
  1.3 1.9 %prepare.1 = (f32[88,128]{1,0:T(8,128)S(1)}, s32[2,128]{1,0:T(2,128)S(1)}) custom-call(f32[2,240]{1,0:T(2,128)} %bitcast.11, f32[2,240]{1,0:T(2,128)} %bitcast.12, f32[2,2,240]{2,1,0:T(2,128)} %bitcast.10, s32[320]{0:T(512)} %from_ref.1, s32[320]{0:T(512)} %to_ref.1, s32[1]{0:T(128)S(6)} %copy.15.count_ref, s32[240]{0:T(256)} %bound_ref.1, f32[320]{0:T(512)} %g_ref.1, ...), custom_call_target="tpu_custom_call" | custom-call | tf_op jit(solution)/shard_map/prepare/pallas_call | solution.py:802
  3.2 3.0 %collective-permute-start = (f32[88,128]{1,0:T(8,128)S(1)}, f32[88,128]{1,0:T(8,128)S(1)}, u32[]{:S(2)}, u32[]{:S(2)}) collective-permute-start(f32[88,128]{1,0:T(8,128)S(1)} %get-tuple-element.7.refs_0_), channel_id=1, source_target_pairs={{0,4},{4,0},{8,12},{12,8},{16,20},{20,16},{24,28},{28,24},{1,5},{5... | collective-permute-start | bytes 135176 | tf_op jit(solution)/shard_map/ppermute | solution.py:832
  6.2 3.6 %collective-permute-start.5 = (f32[88,128]{1,0:T(8,128)S(1)}, f32[88,128]{1,0:T(8,128)S(1)}, u32[]{:S(2)}, u32[]{:S(2)}) collective-permute-start(f32[88,128]{1,0:T(8,128)S(1)} %get-tuple-element.7.refs_0_), channel_id=1, source_target_pairs={{0,24},{4,28},{8,16},{12,20},{16,8},{20,12},{24,0},{28,4},{1,25},{... | collective-permute-start | bytes 135176 | tf_op jit(solution)/shard_map/ppermute | solution.py:832
  9.8 0.0 collective-permute-start.3
  9.8 0.8 %collective-permute-start.1 = (f32[88,128]{1,0:T(8,128)S(1)}, f32[88,128]{1,0:T(8,128)S(1)}, u32[]{:S(2)}, u32[]{:S(2)}) collective-permute-start(f32[88,128]{1,0:T(8,128)S(1)} %get-tuple-element.7.refs_0_), channel_id=1, source_target_pairs={{0,8},{4,12},{8,0},{12,4},{16,24},{20,28},{24,16},{28,20},{1,9},{5... | collective-permute-start | bytes 135176 | tf_op jit(solution)/shard_map/ppermute | solution.py:832
  10.6 0.0 collective-permute-done.refs_1_
  10.6 3.6 %collective-permute-start.6 = (f32[88,128]{1,0:T(8,128)S(1)}, f32[88,128]{1,0:T(8,128)S(1)}, u32[]{:S(2)}, u32[]{:S(2)}) collective-permute-start(f32[88,128]{1,0:T(8,128)S(1)} %collective-permute-done.refs_1_), channel_id=1, source_target_pairs={{0,24},{4,28},{8,16},{12,20},{16,8},{20,12},{24,0},{28,4},{1,25},{... | collective-permute-start | bytes 135176 | tf_op jit(solution)/shard_map/ppermute | solution.py:832
  14.2 0.0 collective-permute-start.4
  14.2 0.0 collective-permute-done.5.refs_6_
  14.2 0.8 %collective-permute-start.2 = (f32[88,128]{1,0:T(8,128)S(1)}, f32[88,128]{1,0:T(8,128)S(1)}, u32[]{:S(2)}, u32[]{:S(2)}) collective-permute-start(f32[88,128]{1,0:T(8,128)S(1)} %collective-permute-done.refs_1_), channel_id=1, source_target_pairs={{0,8},{4,12},{8,0},{12,4},{16,24},{20,28},{24,16},{28,20},{1,9},{5... | collective-permute-start | bytes 135176 | tf_op jit(solution)/shard_map/ppermute | solution.py:832
  15.0 0.8 %collective-permute-done.3.refs_4_ = f32[88,128]{1,0:T(8,128)S(1)} collective-permute-done((f32[88,128]{1,0:T(8,128)S(1)}, f32[88,128]{1,0:T(8,128)S(1)}, u32[]{:S(2)}, u32[]{:S(2)}) %collective-permute-start.3) | collective-permute-done | bytes 45088 | tf_op jit(solution)/shard_map/ppermute | solution.py:832
  15.8 0.0 collective-permute-done.1.refs_2_
  15.8 1.0 %collective-permute-done.6.refs_7_ = f32[88,128]{1,0:T(8,128)S(1)} collective-permute-done((f32[88,128]{1,0:T(8,128)S(1)}, f32[88,128]{1,0:T(8,128)S(1)}, u32[]{:S(2)}, u32[]{:S(2)}) %collective-permute-start.6) | collective-permute-done | bytes 45088 | tf_op jit(solution)/shard_map/ppermute | solution.py:832
  16.8 2.3 %collective-permute-done.4.refs_5_ = f32[88,128]{1,0:T(8,128)S(1)} collective-permute-done((f32[88,128]{1,0:T(8,128)S(1)}, f32[88,128]{1,0:T(8,128)S(1)}, u32[]{:S(2)}, u32[]{:S(2)}) %collective-permute-start.4) | collective-permute-done | bytes 45088 | tf_op jit(solution)/shard_map/ppermute | solution.py:832
  19.2 0.0 collective-permute-done.2.refs_3_
  19.2 3.4 %solve.1 = (f32[2,2,240]{2,1,0:T(2,128)}, f32[2,2,240]{2,1,0:T(2,128)}) custom-call(s32[1]{0:T(128)} %bitcast.me_ref, s32[2,128]{1,0:T(2,128)S(1)} %get-tuple-element.6.pos_ref, f32[88,128]{1,0:T(8,128)S(1)} %get-tuple-element.7.refs_0_, f32[88,128]{1,0:T(8,128)S(1)} %collective-permute-done.refs_1_, f32[88,128]{1,0:T(8,128)S(1)} %collective-permute-done.1.refs_2_, ...), custom_call_target="tpu_custom_call" | custom-call | tf_op jit(solution)/shard_map/solve/pallas_call | solution.py:841
Async XLA Ops:
  3.2 7.4 %collective-permute-start = (f32[88,128]{1,0:T(8,128)S(1)}, f32[88,128]{1,0:T(8,128)S(1)}, u32[]{:S(2)}, u32[]{:S(2)}) collective-permute-start(f32[88,128]{1,0:T(8,128)S(1)} %get-tuple-element.7.refs_0_), channel_id=1, source_target_pairs={{0,4},{4,0},{8,12},{12,8},{16,20},{20,16},{24,28},{28,24},{1,5},{5... | collective-permute-start | bytes 135176 | tf_op jit(solution)/shard_map/ppermute | solution.py:832
  6.2 8.0 %collective-permute-start.5 = (f32[88,128]{1,0:T(8,128)S(1)}, f32[88,128]{1,0:T(8,128)S(1)}, u32[]{:S(2)}, u32[]{:S(2)}) collective-permute-start(f32[88,128]{1,0:T(8,128)S(1)} %get-tuple-element.7.refs_0_), channel_id=1, source_target_pairs={{0,24},{4,28},{8,16},{12,20},{16,8},{20,12},{24,0},{28,4},{1,25},{... | collective-permute-start | bytes 135176 | tf_op jit(solution)/shard_map/ppermute | solution.py:832
  9.8 6.0 %collective-permute-start.3 = (f32[88,128]{1,0:T(8,128)S(1)}, f32[88,128]{1,0:T(8,128)S(1)}, u32[]{:S(2)}, u32[]{:S(2)}) collective-permute-start(f32[88,128]{1,0:T(8,128)S(1)} %get-tuple-element.7.refs_0_), channel_id=1, source_target_pairs={{0,16},{4,20},{8,24},{12,28},{16,0},{20,4},{24,8},{28,12},{1,17},{... | collective-permute-start | bytes 135176 | tf_op jit(solution)/shard_map/ppermute | solution.py:832
  9.8 6.0 %collective-permute-start.1 = (f32[88,128]{1,0:T(8,128)S(1)}, f32[88,128]{1,0:T(8,128)S(1)}, u32[]{:S(2)}, u32[]{:S(2)}) collective-permute-start(f32[88,128]{1,0:T(8,128)S(1)} %get-tuple-element.7.refs_0_), channel_id=1, source_target_pairs={{0,8},{4,12},{8,0},{12,4},{16,24},{20,28},{24,16},{28,20},{1,9},{5... | collective-permute-start | bytes 135176 | tf_op jit(solution)/shard_map/ppermute | solution.py:832
  10.6 6.2 %collective-permute-start.6 = (f32[88,128]{1,0:T(8,128)S(1)}, f32[88,128]{1,0:T(8,128)S(1)}, u32[]{:S(2)}, u32[]{:S(2)}) collective-permute-start(f32[88,128]{1,0:T(8,128)S(1)} %collective-permute-done.refs_1_), channel_id=1, source_target_pairs={{0,24},{4,28},{8,16},{12,20},{16,8},{20,12},{24,0},{28,4},{1,25},{... | collective-permute-start | bytes 135176 | tf_op jit(solution)/shard_map/ppermute | solution.py:832
  14.2 4.9 %collective-permute-start.4 = (f32[88,128]{1,0:T(8,128)S(1)}, f32[88,128]{1,0:T(8,128)S(1)}, u32[]{:S(2)}, u32[]{:S(2)}) collective-permute-start(f32[88,128]{1,0:T(8,128)S(1)} %collective-permute-done.refs_1_), channel_id=1, source_target_pairs={{0,16},{4,20},{8,24},{12,28},{16,0},{20,4},{24,8},{28,12},{1,17},{... | collective-permute-start | bytes 135176 | tf_op jit(solution)/shard_map/ppermute | solution.py:832
  14.2 4.9 %collective-permute-start.2 = (f32[88,128]{1,0:T(8,128)S(1)}, f32[88,128]{1,0:T(8,128)S(1)}, u32[]{:S(2)}, u32[]{:S(2)}) collective-permute-start(f32[88,128]{1,0:T(8,128)S(1)} %collective-permute-done.refs_1_), channel_id=1, source_target_pairs={{0,8},{4,12},{8,0},{12,4},{16,24},{20,28},{24,16},{28,20},{1,9},{5... | collective-permute-start | bytes 135176 | tf_op jit(solution)/shard_map/ppermute | solution.py:832
